TPU v7x, 128 devices: a whole 4x4x4 slice. The times are simulated.
128 devices in a mesh: tile: 32 (over z, y, core), rep: 4 (over x).
Axes of the slice: x: 4, y: 4, z: 4, core: 2. Of those that a mesh axis runs over, the one named last changes fastest.
Arguments:
- amplitudes: bfloat16 [1024, 32, 1024], P('tile'), may hold values from -6 to 6
- integrals: bfloat16 [32, 16, 1024, 1024], P('tile', 'rep'), may hold values from -0.09375 to 0.09375
- owner_order: int32 [32], replicated, may hold values from 0 to 31, each once
- screen_list: int32 [32, 16], replicated, may hold values from 0 to 31, as said below
- live_mask: int32 [32, 16], replicated, may hold values 0 or 1
Outputs:
- ladder: float32 [1024, 32, 1024], P('tile', 'rep')
Inputs may be any that keep to these rules, and one draw needn't show every extreme that they name: `screen_list`: slot s of every row names a tile of block s mod 4, block q holding tiles q * 8 to (q + 1) * 8 - 1.
All inputs are finite; a program needn't handle non-finite values.
Results may differ from a plain program's by a relative error of at most 0.0029.
Values may be sent and summed in bfloat16 or wider, within the bound.
A program may use at most 128 MiB of HBM per device.

v0:
```python
import jax
import jax.numpy as jnp
from jax import lax
from jax.sharding import PartitionSpec as P


def on_device(amplitudes, integrals, owner_order, screen_list, live_mask):
    tile_count = lax.axis_size("tile")
    rep_index = lax.axis_index("rep")
    tile_index = lax.axis_index("tile")
    slot_count = integrals.shape[1]
    pair_width = amplitudes.shape[2]
    row_count = amplitudes.shape[0]
    ordered = jnp.take(amplitudes, owner_order, axis=1)
    column = lax.all_to_all(ordered, "tile", split_axis=1, concat_axis=0, tiled=True)[:, 0, :]
    live_slots = lax.dynamic_slice(
        live_mask, (tile_index, rep_index * slot_count), (1, slot_count)
    )[0]
    pieces = jnp.einsum("mc,scd->msd", column, integrals[0], preferred_element_type=jnp.float32)
    pieces = pieces * live_slots.astype(jnp.float32)[None, :, None]
    grouped = pieces.astype(jnp.bfloat16).reshape(tile_count, row_count, slot_count, pair_width)
    returned = lax.all_to_all(grouped, "tile", split_axis=0, concat_axis=0, tiled=True)
    labels = lax.dynamic_slice_in_dim(screen_list, rep_index * slot_count, slot_count, 1)
    onehot = (labels[:, :, None] == jnp.arange(tile_count, dtype=jnp.int32)[None, None, :]).astype(
        jnp.bfloat16
    )
    dense_sum = jnp.einsum("trkp,tka->rap", returned, onehot, preferred_element_type=jnp.float32)
    return lax.psum_scatter(dense_sum, "rep", scatter_dimension=1, tiled=True)


def solution(mesh):
    in_specs = (P("tile", None, None), P("tile", "rep", None, None), P(), P(), P())
    out_specs = P("tile", "rep", None)
    return jax.shard_map(
        on_device, mesh=mesh, in_specs=in_specs, out_specs=out_specs, check_vma=False
    )
```

profile of v0, /device:TPU:1, one launch (start us, length us, event | category | flops | bytes accessed | tf_op | source)
XLA Modules:
  0.0 251.8 jit_solution(16636741302768016925)
XLA Ops:
  6.5 0.0 copy-start
  6.5 0.8 compare_select_fusion
  7.3 0.7 compare_and_fusion
  8.0 0.1 copy-done
  8.1 7.9 %gather_fusion = bf16[32,32,1024]{2,0,1:T(8,128)(2,1)} fusion(bf16[32,32,1024]{2,1,0:T(8,128)(2,1)S(1)} %copy-done, s32[1024]{0:T(1024)S(1)} %pad_clamp_fusion), kind=kCustom, calls=%fused_computation | custom fusion | bytes 4194432 | tf_op jit(solution)/shard_map/jit(_take)/gather | solution.py:14
  16.0 1.9 select_bitcast_fusion
  17.9 2.5 copy.10
  20.3 9.7 %all-to-all-start = ((bf16[32,32,1024]{2,0,1:T(8,128)(2,1)}), bf16[32,32,1024]{2,0,1:T(8,128)(2,1)}, u32[]{:S(2)}, u32[]{:S(2)}) async-start(bf16[32,32,1024]{2,0,1:T(8,128)(2,1)} %copy.10), calls=%async_computation | async-start | bytes 4194304 | tf_op jit(solution)/shard_map/all_to_all | solution.py:15
  30.0 0.9 convert_reduce_fusion
  30.9 26.9 %all-to-all-done = bf16[32,32,1024]{2,0,1:T(8,128)(2,1)} async-done(((bf16[32,32,1024]{2,0,1:T(8,128)(2,1)}), bf16[32,32,1024]{2,0,1:T(8,128)(2,1)}, u32[]{:S(2)}, u32[]{:S(2)}) %all-to-all-start) | async-done | bytes 2097184 | tf_op jit(solution)/shard_map/all_to_all | solution.py:15
  57.8 12.8 %multiply_convert_fusion = bf16[1024,4,1024]{2,0,1:T(8,128)(2,1)S(1)} fusion(bf16[1024,1024,1]{1,0,2:T(8,128)(2,1)} %bitcast.5, bf16[1,4,1024,1024]{3,2,1,0:T(8,128)(2,1)} %param.6, f32[4]{0:T(128)S(1)} %convert_reduce_fusion), kind=kOutput, calls=%fused_computation.1 | convolution fusion | flops 8598323200 | bytes 18874384 | tf_op jit(solution)/shard_map/mc,scd->msd/dot_general | solution.py:19
  70.6 7.6 %copy.11 = bf16[32,32,4,1024]{3,2,1,0:T(4,128)(2,1)} copy(bf16[32,32,4,1024]{3,1,0,2:T(8,128)(2,1)S(1)} %bitcast.22) | data formatting | bytes 16777216 | tf_op jit(solution)/shard_map/reshape | solution.py:21
  78.2 7.0 %all-to-all-start.1 = ((bf16[32,32,4,1024]{3,2,1,0:T(4,128)(2,1)}), bf16[32,32,4,1024]{3,2,1,0:T(4,128)(2,1)}, u32[]{:S(2)}, u32[]{:S(2)}) async-start(bf16[32,32,4,1024]{3,2,1,0:T(4,128)(2,1)} %copy.11), calls=%async_computation.1 | async-start | bytes 16777216 | tf_op jit(solution)/shard_map/all_to_all | solution.py:22
  85.2 0.0 reduce-scatter.2.cloned.1.call-start
  85.3 0.7 constant_dynamic-slice_fusion
  86.0 99.0 %all-to-all-done.1 = bf16[32,32,4,1024]{3,2,1,0:T(4,128)(2,1)} async-done(((bf16[32,32,4,1024]{3,2,1,0:T(4,128)(2,1)}), bf16[32,32,4,1024]{3,2,1,0:T(4,128)(2,1)}, u32[]{:S(2)}, u32[]{:S(2)}) %all-to-all-start.1) | async-done | bytes 8388640 | tf_op jit(solution)/shard_map/all_to_all | solution.py:22
  185.0 10.4 %fusion.3 = f32[32,32,1024]{2,1,0:T(8,128)} fusion(bf16[32,32,4,1024]{3,2,1,0:T(4,128)(2,1)} %all-to-all-done.1, s32[32,4]{0,1:T(4,128)S(1)} %constant_dynamic-slice_fusion), kind=kOutput, calls=%fused_computation.5 | convolution fusion | flops 268439552 | bytes 12583424 | tf_op jit(solution)/shard_map/trkp,tka->rap/dot_general | solution.py:27
  195.4 0.0 reduce-scatter.2.cloned.1.call-update
  195.5 49.5 %reduce-scatter.2.cloned.1.call-done = f32[32,8,1024]{2,1,0:T(8,128)} async-done(((f32[32,32,1024]{2,1,0:T(8,128)}), f32[32,8,1024]{2,1,0:T(8,128)}) %reduce-scatter.2.cloned.1.call-update) | async-done | bytes 1048592 | tf_op jit(solution)/shard_map/reduce_scatter | solution.py:28
  (1 shorter events, 0.0 us)
Async XLA Ops:
  6.5 1.6 copy-start
  20.3 37.5 %all-to-all-start = ((bf16[32,32,1024]{2,0,1:T(8,128)(2,1)}), bf16[32,32,1024]{2,0,1:T(8,128)(2,1)}, u32[]{:S(2)}, u32[]{:S(2)}) async-start(bf16[32,32,1024]{2,0,1:T(8,128)(2,1)} %copy.10), calls=%async_computation | async-start | bytes 4194304 | tf_op jit(solution)/shard_map/all_to_all | solution.py:15
  78.2 106.8 %all-to-all-start.1 = ((bf16[32,32,4,1024]{3,2,1,0:T(4,128)(2,1)}), bf16[32,32,4,1024]{3,2,1,0:T(4,128)(2,1)}, u32[]{:S(2)}, u32[]{:S(2)}) async-start(bf16[32,32,4,1024]{3,2,1,0:T(4,128)(2,1)} %copy.11), calls=%async_computation.1 | async-start | bytes 16777216 | tf_op jit(solution)/shard_map/all_to_all | solution.py:22
  85.2 159.7 %reduce-scatter.2.cloned.1.call-start = ((), (), s32[]{:S(2)}) async-start(), calls=%async_computation.3 | async-start | bytes 5242880 | tf_op jit(solution)/shard_map/reduce_scatter | solution.py:28
Sparse Core Ops, SparseCore 0:
  195.6 49.2 reduce-scatter.1
where the time goes:
time: 252 us
  waiting for transfers between devices  175 us (69%)
  matrix products  23.2 us (9%)
  local copies, waits for them, and re-layouts  18.8 us (7%)
  starting transfers between devices  16.7 us (7%)
  between operations  13.4 us (5%)
  other arithmetic  4.21 us (2%)
    all_to_all x1, waiting for transfers between devices, on_device(): lax.all_to_all(grouped, 'tile', split_axis=0, concat_axis=0, tiled=True)  99 us
    reduce_scatter x1, waiting for transfers between devices, on_device(): return lax.psum_scatter(dense_sum, 'rep', scatter_dimension=1, tiled=True)  49.5 us
    all_to_all x1, waiting for transfers between devices, on_device(): lax.all_to_all(ordered, 'tile', split_axis=1, concat_axis=0, tiled=True)  26.9 us
    dot_general x1, matrix products, on_device(): jnp.einsum('mc,scd->msd', column, integrals[0], preferred_element_type=jn...  12.8 us
    dot_general x1, matrix products, on_device(): jnp.einsum('trkp,tka->rap', returned, onehot, preferred_element_type=jnp....  10.4 us
    all_to_all x1, starting transfers between devices, on_device(): lax.all_to_all(ordered, 'tile', split_axis=1, concat_axis=0, tiled=True)  9.67 us
    gather x1, local copies, waits for them, and re-layouts, on_device(): ordered = jnp.take(amplitudes, owner_order, axis=1)  7.88 us
    reshape x1, local copies, waits for them, and re-layouts, on_device(): pieces.astype(jnp.bfloat16)  7.65 us
  transfers between devices with their start and end apart: 3, of which 3 were waited for; matrix products, arithmetic and copies ran while one was open for 1% of the time, Pallas kernels for 0%

commit v1 on v0

v1 whole, which is shorter than its diff:
```python
import functools

import jax
import jax.numpy as jnp
from jax import lax
from jax.experimental import pallas as pl
from jax.experimental.pallas import tpu as pltpu
from jax.sharding import PartitionSpec as P

MESH = pl.DeviceIdType.MESH
BF16, F32, I32 = jnp.bfloat16, jnp.float32, jnp.int32
NAT = ("x1", "x0", "z1", "z0", "y1", "y0")
ORDER = ("x0", "y0", "z0", "x1", "y1", "z1")
STREAMS = ((0, 0, 384), (0, 384, 384), (0, 768, 256), (1, 0, 384), (1, 384, 384), (1, 768, 256))


def bits_of(r):
    return [ORDER[(r + i) % 6] for i in range(6)]


def last_z(r):
    return [b for b in bits_of(r) if b[0] == "z"][1]


def gray(v):
    return v + v // 2 - 2 * (v // 3)


def left(r, used):
    gone = bits_of(r)[:used]
    return [b for b in NAT if b not in gone]


def view(ref, lead, names, fixed, tail=()):
    return ref.at[tuple(lead) + tuple(fixed[b] if b in fixed else slice(None) for b in names) + tuple(tail)]


def kernel(owner, screen, live, amp_hbm, int_hbm, out, amp, ints, ordered, column, pieces, weights, *rest):
    r1, r2, r3, s4, r4, k4, s5, r5, k5, s6, r6 = (rest[6 * i : 6 * i + 6] for i in range(11))
    load_sem, amp_sem, send_sem, sem1, sem2, sem3, sem4, sem5, sem6 = rest[66:]
    x, t = lax.axis_index("rep"), lax.axis_index("tile")
    z, y, c = t // 8, (t // 2) % 4, t % 2
    g = {"x": gray(x), "y": gray(y), "z": gray(z)}
    mine = {a + "1": g[a] // 2 for a in g} | {a + "0": g[a] % 2 for a in g}
    other = {b: 1 - mine[b] for b in mine}

    def device(flips, core):
        at = {a: gray((other if a + "1" in flips else mine)[a + "1"] * 2 + (other if a + "0" in flips else mine)[a + "0"]) for a in g}
        return (at["z"] * 8 + at["y"] * 2 + core, at["x"])

    sent = []

    def send(src, dst, sem, to):
        copy = pltpu.make_async_remote_copy(src, dst, send_sem, sem, device_id=to, device_id_type=MESH)
        copy.start()
        sent.append(copy)

    def wait(ref, sem):
        pltpu.make_async_copy(ref, ref, sem).wait()

    load_amp = pltpu.make_async_copy(amp_hbm, amp, load_sem.at[0])
    load_amp.start()
    load_ints = [pltpu.make_async_copy(int_hbm.at[j], ints.at[j], load_sem.at[1 + j]) for j in range(4)]
    for load in load_ints:
        load.start()

    barrier = pltpu.get_barrier_semaphore()

    @pl.loop(1, 32)
    def _(k):
        to = ((z + k // 8) % 4) * 8 + ((y + (k // 2) % 4) % 4) * 2 + (c + k) % 2
        pl.semaphore_signal(barrier, inc=1, device_id=(to, x), device_id_type=MESH)

    for b in ("x0", "x1"):
        for core in range(2):
            pl.semaphore_signal(barrier, inc=1, device_id=device((b,), core), device_id_type=MESH)

    lane = lax.broadcasted_iota(I32, (8, 256), 1)
    bin_of_row = lax.broadcasted_iota(I32, (8, 256), 0)
    for r in range(6):
        e = bits_of(r)
        x_left = [b for b in e[3:] if b[0] == "x"][0]
        for f in range(2):
            want = dict(mine)
            if f:
                want[x_left] = other[x_left]
            block = gray(want["x1"] * 2 + want["x0"])
            label = jnp.full((8, 256), -1, I32)
            for s in range(16):
                flips = [e[2 - i] for i in range(3) if (s >> (3 - i)) & 1]
                tile, rep = device(flips, s & 1)
                slot = rep * 4 + block
                found = jnp.where(live[tile, slot] != 0, screen[tile, slot] - 8 * block, -1)
                label = jnp.where(lane // 16 == s, found, label)
            hit = label == bin_of_row
            rows = [jnp.where(hit & (lane % 16 == m), 1.0, 0.0).astype(F32) for m in range(16)]
            weights[2 * r + f] = jnp.concatenate(rows, axis=0).astype(BF16)

    load_amp.wait()
    away = lax.broadcasted_iota(I32, (32, 1024), 1) - 32 * lax.broadcasted_iota(I32, (32, 1024), 0)

    @pl.loop(0, 4)
    def _(zz):
        pick = [jnp.where(away == owner[zz * 8 + i], 1.0, 0.0).astype(BF16) for i in range(8)]
        pick = jnp.concatenate(pick, axis=0)
        for n in range(2):
            got = jnp.dot(pick, amp[:, n * 512 : n * 512 + 512], preferred_element_type=F32)
            ordered[pl.ds(zz * 8, 8), :, n * 512 : n * 512 + 512] = got.astype(BF16).reshape(8, 32, 512)

    pl.semaphore_wait(barrier, 35)

    own_row = g["y"] * 2 + c
    own = pltpu.make_async_copy(ordered.at[t], column.at[g["z"], own_row], amp_sem.at[g["z"]])
    own.start()

    def amp_copy(dz, dy, dc):
        to = ((z + dz) % 4) * 8 + ((y + dy) % 4) * 2 + (c + dc) % 2
        send(ordered.at[to], column.at[g["z"], own_row], amp_sem.at[g["z"]], (to, x))

    for dz in (0, 1, 3, 2):
        for dy in (0, 1, 3, 2):
            for dc in (0, 1):
                if (dz, dy, dc) != (0, 0, 0):
                    amp_copy(dz, dy, dc)

    for load in load_ints:
        load.wait()

    slot_of = (0, 1, 3, 2)
    for k in range(4):
        zv = {"z1": (other if k >> 1 else mine)["z1"], "z0": (other if k & 1 else mine)["z0"]}
        gz = zv["z1"] * 2 + zv["z0"]
        wait(column.at[gz], amp_sem.at[gz])

        @pl.loop(0, 8)
        def _(step):
            j, cols = step // 2, pl.ds(pl.multiple_of((step % 2) * 512, 512), 512)
            left_side = column[gz].reshape(256, 1024)
            got = jnp.dot(left_side, ints[j, :, cols], preferred_element_type=F32).astype(BF16)
            gj = gray(j)
            pieces[gj // 2, gj % 2, zv["z1"], zv["z0"], :, :, :, :, :, cols] = got.reshape(2, 2, 2, 2, 16, 512)

        for r, (h, start, width) in enumerate(STREAMS):
            e1, zl = bits_of(r)[0], last_z(r)
            v = k >> 1 if zl == "z1" else k & 1
            sem = sem1.at[r, v]
            cols = pl.ds(start, width)
            flip_z = {"z0": k & 1, "z1": k >> 1}
            names = left(r, 1)

            def part(e1_value, core):
                return view(pieces, (), NAT, {e1: e1_value} | zv, (core, h, slice(None), cols))

            def place(a):
                return view(r1[r], (a, c), names, {b: n for b, n in zv.items() if b != e1})

            if e1[0] != "z" or flip_z[e1]:
                for core in range(2):
                    send(part(other[e1], core), place(1), sem, device((e1,), core))
            if e1[0] != "z" or not flip_z[e1]:
                send(part(mine[e1], 1 - c), place(0), sem, device((), 1 - c))
                pltpu.make_async_copy(part(mine[e1], c), place(0), sem).start()

    def zfix(r, v):
        zl = last_z(r)
        return {zl: (other if v else mine)[zl]}

    for v in range(2):
        for r in range(6):
            e1, e2, e3 = bits_of(r)[:3]
            fix = zfix(r, v)
            wait(view(r1[r], (slice(None), slice(None)), left(r, 1), fix), sem1.at[r, v])
            send(
                view(r1[r], (slice(None), slice(None)), left(r, 1), {e2: other[e2]} | fix),
                view(r2[r], (slice(None), slice(None)), left(r, 2), fix),
                sem2.at[r, v],
                device((e2,), c),
            )
            send(
                view(r1[r], (slice(None), slice(None)), left(r, 1), {e2: mine[e2], e3: other[e3]} | fix),
                view(r3[r], (0, slice(None), slice(None)), left(r, 3), fix),
                sem3.at[r, v],
                device((e3,), c),
            )
    for v in range(2):
        for r in range(6):
            e1, e2, e3 = bits_of(r)[:3]
            fix = zfix(r, v)
            wait(view(r2[r], (slice(None), slice(None)), left(r, 2), fix), sem2.at[r, v])
            send(
                view(r2[r], (slice(None), slice(None)), left(r, 2), {e3: other[e3]} | fix),
                view(r3[r], (1, slice(None), slice(None)), left(r, 3), fix),
                sem3.at[r, v],
                device((e3,), c),
            )

    def zlast_at(r):
        return bits_of(r).index(last_z(r)) - 3

    for v in range(2):
        for r in range(6):
            e = bits_of(r)
            fix = zfix(r, v)
            wait(view(r3[r], (slice(None),) * 3, left(r, 3), fix), sem3.at[r, v])
            at = zlast_at(r)
            for code in range(8):
                f = (code >> 2, (code >> 1) & 1, code & 1)
                if f[at] != v:
                    continue
                here = {b: (other if n else mine)[b] for b, n in zip(e[3:], f)}
                all_here = here | {e[1]: mine[e[1]], e[2]: mine[e[2]]}
                blocks = []
                for a in range(2):
                    for core in range(2):
                        blocks.append(r1[r][(a, core) + tuple(all_here[b] for b in left(r, 1))])
                for a in range(2):
                    for core in range(2):
                        blocks.append(r2[r][(a, core) + tuple(all_here[b] for b in left(r, 2))])
                for b2 in range(2):
                    for a in range(2):
                        for core in range(2):
                            blocks.append(r3[r][(b2, a, core) + tuple(all_here[b] for b in left(r, 3))])
                x_at = [b[0] for b in e[3:]].index("x")
                binned = jnp.dot(weights[2 * r + f[x_at]], jnp.concatenate(blocks, axis=0), preferred_element_type=F32)
                if f[0]:
                    s4[r][f[1], f[2]] = binned.astype(BF16)
                else:
                    k4[r][f[1], f[2]] = binned
            to = device((e[3],), c)
            if at == 2:
                send(s4[r].at[:, v], r4[r].at[:, v], sem4.at[r, v], to)
            elif at == 1:
                send(s4[r].at[v], r4[r].at[v], sem4.at[r, v], to)
            elif v == 1:
                send(s4[r], r4[r], sem4.at[r, 0], to)

    def step5(r, f5, f6):
        total = k4[r][f5, f6] + r4[r][f5, f6].astype(F32)
        if f5:
            s5[r][f6] = total.astype(BF16)
        else:
            k5[r][f6] = total

    for v in range(2):
        for r in range(6):
            at = zlast_at(r)
            to = device((bits_of(r)[4],), c)
            if at == 2:
                wait(r4[r].at[:, v], sem4.at[r, v])
                step5(r, 1, v)
                send(s5[r].at[v], r5[r].at[v], sem5.at[r, v], to)
                step5(r, 0, v)
            elif at == 1:
                u = 1 - v
                wait(r4[r].at[u], sem4.at[r, u])
                step5(r, u, 0)
                step5(r, u, 1)
                if u:
                    send(s5[r], r5[r], sem5.at[r, 0], to)
            elif v == 1:
                wait(r4[r], sem4.at[r, 0])
                step5(r, 1, 0)
                step5(r, 1, 1)
                send(s5[r], r5[r], sem5.at[r, 0], to)
                step5(r, 0, 0)
                step5(r, 0, 1)

    for r in range(6):
        if zlast_at(r) == 2:
            wait(r5[r].at[1], sem5.at[r, 1])
        else:
            wait(r5[r], sem5.at[r, 0])
        s6[r][...] = (k5[r][1] + r5[r][1].astype(F32)).astype(BF16)
        send(s6[r], r6[r], sem6.at[r], device((bits_of(r)[5],), c))
    for r, (h, start, width) in enumerate(STREAMS):
        if zlast_at(r) == 2:
            wait(r5[r].at[0], sem5.at[r, 0])
        wait(r6[r], sem6.at[r])
        total = k5[r][0] + r5[r][0].astype(F32) + r6[r][...].astype(F32)
        out[16 * h : 16 * h + 16, :, start : start + width] = total.reshape(16, 8, width)

    for copy in sent:
        copy.wait_send()


def on_device(amplitudes, integrals, owner_order, screen_list, live_mask):
    rows, tiles, width = amplitudes.shape
    widths = [w for _, _, w in STREAMS]

    def group(lead, tail, dtype):
        return [pltpu.VMEM(lead + tail(w), dtype) for w in widths]

    two = (2,)
    raw = lambda w: (16, w)
    dense = lambda w: (128, w)
    scratch = [
        pltpu.VMEM((rows * tiles, width), BF16),
        pltpu.VMEM((4, width, width), BF16),
        pltpu.VMEM((tiles, rows, width), BF16),
        pltpu.VMEM((4, 8, rows, width), BF16),
        pltpu.VMEM(two * 8 + (16, width), BF16),
        pltpu.VMEM((12, 128, 256), BF16),
        *group(two * 7, raw, BF16),
        *group(two * 6, raw, BF16),
        *group(two * 6, raw, BF16),
        *group(two * 2, dense, BF16),
        *group(two * 2, dense, BF16),
        *group(two * 2, dense, F32),
        *group(two, dense, BF16),
        *group(two, dense, BF16),
        *group(two, dense, F32),
        *group((), dense, BF16),
        *group((), dense, BF16),
        pltpu.SemaphoreType.DMA((5,)),
        pltpu.SemaphoreType.DMA((4,)),
        pltpu.SemaphoreType.DMA,
        *[pltpu.SemaphoreType.DMA((6, 2))] * 5,
        pltpu.SemaphoreType.DMA((6,)),
    ]
    smem = pl.BlockSpec(memory_space=pltpu.SMEM)
    hbm = pl.BlockSpec(memory_space=pl.ANY)
    return pl.pallas_call(
        kernel,
        out_shape=jax.ShapeDtypeStruct((rows, 8, width), F32),
        in_specs=[smem, smem, smem, hbm, hbm],
        out_specs=pl.BlockSpec(memory_space=pltpu.VMEM),
        scratch_shapes=scratch,
        cost_estimate=pl.CostEstimate(flops=13_000_000_000, bytes_accessed=12 << 20, transcendentals=0),
        compiler_params=pltpu.CompilerParams(
            collective_id=0, has_side_effects=True, vmem_limit_bytes=60 << 20
        ),
    )(owner_order, screen_list, live_mask, amplitudes.reshape(rows * tiles, width), integrals[0])


def solution(mesh):
    in_specs = (P("tile", None, None), P("tile", "rep", None, None), P(), P(), P())
    out_specs = P("tile", "rep", None)
    return jax.shard_map(
        on_device, mesh=mesh, in_specs=in_specs, out_specs=out_specs, check_vma=False
    )
```

time: 252 us -> 113 us (0.45)
  waiting for transfers between devices: 175 us -> 0 us
  Pallas kernels: 0 us -> 107 us
  matrix products: 23.2 us -> 0 us
  starting transfers between devices: 16.7 us -> 0 us
  local copies, waits for them, and re-layouts: 18.8 us -> 5.05 us
  between operations: 13.4 us -> 0.01 us
  other arithmetic: 4.21 us -> 0 us
    all_to_all x2 -> x0, waiting for transfers between devices: 126 us -> none  [the longest x1 99 us: on_device(): lax.all_to_all(grouped, 'tile', split_axis=0, concat_axis=0, tiled=True)]
    pallas_call x0 -> x1, Pallas kernels: none -> 107 us  [on_device(): pl.pallas_call(kernel, out_shape=jax.ShapeDtypeStruct((rows, 8, width), F...]
    reduce_scatter x1 -> x0, waiting for transfers between devices: 49.5 us -> none  [on_device(): return lax.psum_scatter(dense_sum, 'rep', scatter_dimension=1, tiled=True)]
    dot_general x2 -> x0, matrix products: 23.2 us -> none  [the longest x1 12.8 us: on_device(): jnp.einsum('mc,scd->msd', column, integrals[0], preferred_element_type=jn...]
    all_to_all x2 -> x0, starting transfers between devices: 16.7 us -> none  [the longest x1 9.67 us: on_device(): lax.all_to_all(ordered, 'tile', split_axis=1, concat_axis=0, tiled=True)]
    gather x1 -> x0, local copies, waits for them, and re-layouts: 7.88 us -> none  [on_device(): ordered = jnp.take(amplitudes, owner_order, axis=1)]
    reshape x1 -> x0, local copies, waits for them, and re-layouts: 7.65 us -> none  [on_device(): pieces.astype(jnp.bfloat16)]
    unnamed x2 -> x3, local copies, waits for them, and re-layouts: 0.13 us -> 5.05 us
  transfers between devices with their start and end apart: 3 -> 0, of which waited for: 3 -> 0; matrix products, arithmetic and copies ran while one was open for 1% -> 0% of each run, Pallas kernels for 0% -> 0%
where the time goes in v1:
time: 113 us; the launch traced here: 112 us
  Pallas kernels  107 us (95%)
  local copies, waits for them, and re-layouts  5.05 us (4%)
    pallas_call x1, Pallas kernels, on_device(): pl.pallas_call(kernel, out_shape=jax.ShapeDtypeStruct((rows, 8, width), F...  107 us
    unnamed x3, local copies, waits for them, and re-layouts  5.05 us

profile of v1, /device:TPU:1, one launch (start us, length us, event | category | flops | bytes accessed | tf_op | source)
XLA Modules:
  0.0 112.4 jit_solution(8742621216332779469)
XLA Ops:
  0.0 1.4 %copy.6.screen = s32[32,16]{1,0:T(8,128)} copy(s32[32,16]{0,1:T(8,128)} %param.8) | data formatting | bytes 4096 | tf_op args[3]
  1.4 1.4 %copy.7.live = s32[32,16]{1,0:T(8,128)} copy(s32[32,16]{0,1:T(8,128)} %param.9) | data formatting | bytes 4096 | tf_op args[4]
  2.7 107.3 %shard_map.55 = f32[32,8,1024]{2,1,0:T(8,128)} custom-call(s32[32]{0:T(128)} %owner.1, s32[32,16]{1,0:T(8,128)} %copy.6.screen, s32[32,16]{1,0:T(8,128)} %copy.7.live, bf16[1024,1024]{1,0:T(8,128)(2,1)} %bitcast.3, bf16[4,1024,1024]{2,1,0:T(8,128)(2,1)} %bitcast.2), custom_call_target="tpu_custom_call" | custom-call | flops 12999999488 | bytes 12582912 | tf_op jit(solution)/shard_map/pallas_call | solution.py:322
  110.1 2.3 %copy.9 = f32[32,8,1024]{2,1,0:T(8,128)} copy(f32[32,8,1024]{2,1,0:T(8,128)} %shard_map.55) | data formatting | bytes 2097152

commit v2 on v1

--- a/solution.py
+++ b/solution.py
@@ -12,6 +12,7 @@
 NAT = ("x1", "x0", "z1", "z0", "y1", "y0")
 ORDER = ("x0", "y0", "z0", "x1", "y1", "z1")
 STREAMS = ((0, 0, 384), (0, 384, 384), (0, 768, 256), (1, 0, 384), (1, 384, 384), (1, 768, 256))
+CHUNKS, HALVES = (1, 2, 3, 0), (1, 0)
 
 
 def bits_of(r):
@@ -37,7 +38,7 @@
 
 def kernel(owner, screen, live, amp_hbm, int_hbm, out, amp, ints, ordered, column, pieces, weights, *rest):
     r1, r2, r3, s4, r4, k4, s5, r5, k5, s6, r6 = (rest[6 * i : 6 * i + 6] for i in range(11))
-    load_sem, amp_sem, send_sem, sem1, sem2, sem3, sem4, sem5, sem6 = rest[66:]
+    load_sem, amp_sem, far_sem, send_sem, sem1, sem2, sem3, sem4, sem5, sem6 = rest[66:]
     x, t = lax.axis_index("rep"), lax.axis_index("tile")
     z, y, c = t // 8, (t // 2) % 4, t % 2
     g = {"x": gray(x), "y": gray(y), "z": gray(z)}
@@ -61,8 +62,6 @@
     load_amp = pltpu.make_async_copy(amp_hbm, amp, load_sem.at[0])
     load_amp.start()
     load_ints = [pltpu.make_async_copy(int_hbm.at[j], ints.at[j], load_sem.at[1 + j]) for j in range(4)]
-    for load in load_ints:
-        load.start()
 
     barrier = pltpu.get_barrier_semaphore()
 
@@ -74,6 +73,36 @@
     for b in ("x0", "x1"):
         for core in range(2):
             pl.semaphore_signal(barrier, inc=1, device_id=device((b,), core), device_id_type=MESH)
+    pl.semaphore_signal(barrier, inc=1, device_id=device(("x0", "x1"), c), device_id_type=MESH)
+
+    def far(n):
+        return ((2, x // 2), (2, 2 + x // 2), (1, 2 - x // 2), (3, 2 + x // 2))[n] + (x % 2,)
+
+    load_amp.wait()
+    for load in load_ints:
+        load.start()
+    away = lax.broadcasted_iota(I32, (32, 1024), 1) - 32 * lax.broadcasted_iota(I32, (32, 1024), 0)
+    own_row = g["y"] * 2 + c
+    near = [(dz, dy, dc) for dz, dy in ((1, 0), (1, 3), (3, 0), (3, 1), (0, 1), (0, 3), (0, 0), (0, 2)) for dc in (0, 1)]
+    blocks = [far(n) for n in (2, 3, 0, 1)] + near
+    for first in (0, 8, 16):
+        some = blocks[first : first + 8]
+        to = [((z + dz) % 4) * 8 + ((y + dy) % 4) * 2 + (c + dc) % 2 for dz, dy, dc in some]
+        pick = [jnp.where(away == owner[p], 1.0, 0.0).astype(BF16) for p in to]
+        pick = jnp.concatenate(pick, axis=0)
+        for n in range(2):
+            got = jnp.dot(pick, amp[:, n * 512 : n * 512 + 512], preferred_element_type=F32)
+            ordered[first : first + len(some), :, n * 512 : n * 512 + 512] = got.astype(BF16).reshape(len(some), 32, 512)
+        if first == 0:
+            pl.semaphore_wait(barrier, 36)
+        for i, p in enumerate(to):
+            src, dst = ordered.at[first + i], column.at[g["z"], own_row]
+            if some[i] == (0, 0, 0):
+                pltpu.make_async_copy(src, dst, amp_sem.at[g["z"]]).start()
+            elif first == 0 and i < 4:
+                send(src, dst, far_sem.at[(2, 3, 0, 1)[i]], (p, x))
+            else:
+                send(src, dst, amp_sem.at[g["z"]], (p, x))
 
     lane = lax.broadcasted_iota(I32, (8, 256), 1)
     bin_of_row = lax.broadcasted_iota(I32, (8, 256), 0)
@@ -90,55 +119,34 @@
                 flips = [e[2 - i] for i in range(3) if (s >> (3 - i)) & 1]
                 tile, rep = device(flips, s & 1)
                 slot = rep * 4 + block
-                found = jnp.where(live[tile, slot] != 0, screen[tile, slot] - 8 * block, -1)
+                found = jnp.where(live[slot, tile] != 0, screen[slot, tile] - 8 * block, -1)
                 label = jnp.where(lane // 16 == s, found, label)
             hit = label == bin_of_row
             rows = [jnp.where(hit & (lane % 16 == m), 1.0, 0.0).astype(F32) for m in range(16)]
             weights[2 * r + f] = jnp.concatenate(rows, axis=0).astype(BF16)
 
-    load_amp.wait()
-    away = lax.broadcasted_iota(I32, (32, 1024), 1) - 32 * lax.broadcasted_iota(I32, (32, 1024), 0)
-
-    @pl.loop(0, 4)
-    def _(zz):
-        pick = [jnp.where(away == owner[zz * 8 + i], 1.0, 0.0).astype(BF16) for i in range(8)]
-        pick = jnp.concatenate(pick, axis=0)
-        for n in range(2):
-            got = jnp.dot(pick, amp[:, n * 512 : n * 512 + 512], preferred_element_type=F32)
-            ordered[pl.ds(zz * 8, 8), :, n * 512 : n * 512 + 512] = got.astype(BF16).reshape(8, 32, 512)
-
-    pl.semaphore_wait(barrier, 35)
-
-    own_row = g["y"] * 2 + c
-    own = pltpu.make_async_copy(ordered.at[t], column.at[g["z"], own_row], amp_sem.at[g["z"]])
-    own.start()
-
-    def amp_copy(dz, dy, dc):
-        to = ((z + dz) % 4) * 8 + ((y + dy) % 4) * 2 + (c + dc) % 2
-        send(ordered.at[to], column.at[g["z"], own_row], amp_sem.at[g["z"]], (to, x))
-
-    for dz in (0, 1, 3, 2):
-        for dy in (0, 1, 3, 2):
-            for dc in (0, 1):
-                if (dz, dy, dc) != (0, 0, 0):
-                    amp_copy(dz, dy, dc)
+    for n in (2, 3, 0, 1):
+        dz, dy, dc = far(n)
+        gz = gray((z - dz + 4) % 4)
+        block = column.at[gz, gray((y - dy + 4) % 4) * 2 + (c + dc) % 2]
+        wait(block, far_sem.at[n])
+        for dx in (1, 3, 2):
+            send(block, block, amp_sem.at[gz], (t, (x + dx) % 4))
 
     for load in load_ints:
         load.wait()
 
-    slot_of = (0, 1, 3, 2)
-    for k in range(4):
+    for k in CHUNKS:
         zv = {"z1": (other if k >> 1 else mine)["z1"], "z0": (other if k & 1 else mine)["z0"]}
         gz = zv["z1"] * 2 + zv["z0"]
-        wait(column.at[gz], amp_sem.at[gz])
-
-        @pl.loop(0, 8)
-        def _(step):
-            j, cols = step // 2, pl.ds(pl.multiple_of((step % 2) * 512, 512), 512)
+        wait(column.at[gz, pl.ds(0, (8, 7, 7, 6)[k])], amp_sem.at[gz])
+
+        @pl.loop(0, 4)
+        def _(j):
             left_side = column[gz].reshape(256, 1024)
-            got = jnp.dot(left_side, ints[j, :, cols], preferred_element_type=F32).astype(BF16)
+            got = jnp.dot(left_side, ints[j], preferred_element_type=F32).astype(BF16)
             gj = gray(j)
-            pieces[gj // 2, gj % 2, zv["z1"], zv["z0"], :, :, :, :, :, cols] = got.reshape(2, 2, 2, 2, 16, 512)
+            pieces[gj // 2, gj % 2, zv["z1"], zv["z0"]] = got.reshape(2, 2, 2, 2, 16, 1024)
 
         for r, (h, start, width) in enumerate(STREAMS):
             e1, zl = bits_of(r)[0], last_z(r)
@@ -165,7 +173,7 @@
         zl = last_z(r)
         return {zl: (other if v else mine)[zl]}
 
-    for v in range(2):
+    for v in HALVES:
         for r in range(6):
             e1, e2, e3 = bits_of(r)[:3]
             fix = zfix(r, v)
@@ -182,7 +190,7 @@
                 sem3.at[r, v],
                 device((e3,), c),
             )
-    for v in range(2):
+    for v in HALVES:
         for r in range(6):
             e1, e2, e3 = bits_of(r)[:3]
             fix = zfix(r, v)
@@ -197,7 +205,7 @@
     def zlast_at(r):
         return bits_of(r).index(last_z(r)) - 3
 
-    for v in range(2):
+    for v in HALVES:
         for r in range(6):
             e = bits_of(r)
             fix = zfix(r, v)
@@ -241,7 +249,7 @@
         else:
             k5[r][f6] = total
 
-    for v in range(2):
+    for v in HALVES:
         for r in range(6):
             at = zlast_at(r)
             to = device((bits_of(r)[4],), c)
@@ -296,7 +304,7 @@
     scratch = [
         pltpu.VMEM((rows * tiles, width), BF16),
         pltpu.VMEM((4, width, width), BF16),
-        pltpu.VMEM((tiles, rows, width), BF16),
+        pltpu.VMEM((20, rows, width), BF16),
         pltpu.VMEM((4, 8, rows, width), BF16),
         pltpu.VMEM(two * 8 + (16, width), BF16),
         pltpu.VMEM((12, 128, 256), BF16),
@@ -312,6 +320,7 @@
         *group((), dense, BF16),
         *group((), dense, BF16),
         pltpu.SemaphoreType.DMA((5,)),
+        pltpu.SemaphoreType.DMA((4,)),
         pltpu.SemaphoreType.DMA((4,)),
         pltpu.SemaphoreType.DMA,
         *[pltpu.SemaphoreType.DMA((6, 2))] * 5,
@@ -329,7 +338,7 @@
         compiler_params=pltpu.CompilerParams(
             collective_id=0, has_side_effects=True, vmem_limit_bytes=60 << 20
         ),
-    )(owner_order, screen_list, live_mask, amplitudes.reshape(rows * tiles, width), integrals[0])
+    )(owner_order, screen_list.T, live_mask.T, amplitudes.reshape(rows * tiles, width), integrals[0])
 
 
 def solution(mesh):

time: 113 us -> 98.7 us (0.87)
  Pallas kernels: 107 us -> 96.2 us
  local copies, waits for them, and re-layouts: 5.05 us -> 2.31 us
    pallas_call x1, Pallas kernels: 107 us -> 96.2 us  [on_device(): pl.pallas_call(kernel, out_shape=jax.ShapeDtypeStruct((rows, 8, width), F...]
    unnamed x3 -> x1, local copies, waits for them, and re-layouts: 5.05 us -> 2.31 us
where the time goes in v2:
time: 98.7 us; the launch traced here: 98.5 us
  Pallas kernels  96.2 us (97%)
  local copies, waits for them, and re-layouts  2.31 us (2%)
    pallas_call x1, Pallas kernels, on_device(): pl.pallas_call(kernel, out_shape=jax.ShapeDtypeStruct((rows, 8, width), F...  96.2 us
    unnamed x1, local copies, waits for them, and re-layouts  2.31 us

profile of v2, /device:TPU:1, one launch (start us, length us, event | category | flops | bytes accessed | tf_op | source)
XLA Modules:
  0.0 98.5 jit_solution(3435747683566403605)
XLA Ops:
  0.0 96.2 %shard_map.55 = f32[32,8,1024]{2,1,0:T(8,128)} custom-call(s32[32]{0:T(128)} %owner.1, s32[16,32]{1,0:T(8,128)} %bitcast.6, s32[16,32]{1,0:T(8,128)} %bitcast.7, bf16[1024,1024]{1,0:T(8,128)(2,1)} %bitcast.5, bf16[4,1024,1024]{2,1,0:T(8,128)(2,1)} %bitcast.4), custom_call_target="tpu_custom_call" | custom-call | flops 12999999488 | bytes 12582912 | tf_op jit(solution)/shard_map/pallas_call | solution.py:331
  96.2 2.3 %copy.7 = f32[32,8,1024]{2,1,0:T(8,128)} copy(f32[32,8,1024]{2,1,0:T(8,128)} %shard_map.55) | data formatting | bytes 2097152

commit v3 on v2

--- a/solution.py
+++ b/solution.py
@@ -12,7 +12,7 @@
 NAT = ("x1", "x0", "z1", "z0", "y1", "y0")
 ORDER = ("x0", "y0", "z0", "x1", "y1", "z1")
 STREAMS = ((0, 0, 384), (0, 384, 384), (0, 768, 256), (1, 0, 384), (1, 384, 384), (1, 768, 256))
-CHUNKS, HALVES = (1, 2, 3, 0), (1, 0)
+CHUNKS = (1, 2, 3, 0)
 
 
 def bits_of(r):
@@ -169,119 +169,128 @@
                 send(part(mine[e1], 1 - c), place(0), sem, device((), 1 - c))
                 pltpu.make_async_copy(part(mine[e1], c), place(0), sem).start()
 
-    def zfix(r, v):
-        zl = last_z(r)
-        return {zl: (other if v else mine)[zl]}
-
-    for v in HALVES:
+    def keys(r):
+        e, zl = bits_of(r), last_z(r)
+        return (zl, e[4]) if zl == e[3] else (zl, e[3])
+
+    def pick_part(r, v, u):
+        first, second = keys(r)
+        return {first: (other if v else mine)[first], second: (other if u else mine)[second]}
+
+    every = slice(None)
+    for v in (1, 0):
         for r in range(6):
             e1, e2, e3 = bits_of(r)[:3]
-            fix = zfix(r, v)
-            wait(view(r1[r], (slice(None), slice(None)), left(r, 1), fix), sem1.at[r, v])
-            send(
-                view(r1[r], (slice(None), slice(None)), left(r, 1), {e2: other[e2]} | fix),
-                view(r2[r], (slice(None), slice(None)), left(r, 2), fix),
-                sem2.at[r, v],
-                device((e2,), c),
-            )
-            send(
-                view(r1[r], (slice(None), slice(None)), left(r, 1), {e2: mine[e2], e3: other[e3]} | fix),
-                view(r3[r], (0, slice(None), slice(None)), left(r, 3), fix),
-                sem3.at[r, v],
-                device((e3,), c),
-            )
-    for v in HALVES:
+            zl = last_z(r)
+            wait(view(r1[r], (every, every), left(r, 1), {zl: (other if v else mine)[zl]}), sem1.at[r, v])
+            for u in (1, 0):
+                fix = pick_part(r, v, u)
+                send(
+                    view(r1[r], (every, every), left(r, 1), {e2: other[e2]} | fix),
+                    view(r2[r], (every, every), left(r, 2), fix),
+                    sem2.at[r, 2 * v + u],
+                    device((e2,), c),
+                )
         for r in range(6):
             e1, e2, e3 = bits_of(r)[:3]
-            fix = zfix(r, v)
-            wait(view(r2[r], (slice(None), slice(None)), left(r, 2), fix), sem2.at[r, v])
-            send(
-                view(r2[r], (slice(None), slice(None)), left(r, 2), {e3: other[e3]} | fix),
-                view(r3[r], (1, slice(None), slice(None)), left(r, 3), fix),
-                sem3.at[r, v],
-                device((e3,), c),
-            )
-
-    def zlast_at(r):
-        return bits_of(r).index(last_z(r)) - 3
-
-    for v in HALVES:
-        for r in range(6):
-            e = bits_of(r)
-            fix = zfix(r, v)
-            wait(view(r3[r], (slice(None),) * 3, left(r, 3), fix), sem3.at[r, v])
-            at = zlast_at(r)
-            for code in range(8):
-                f = (code >> 2, (code >> 1) & 1, code & 1)
-                if f[at] != v:
-                    continue
-                here = {b: (other if n else mine)[b] for b, n in zip(e[3:], f)}
-                all_here = here | {e[1]: mine[e[1]], e[2]: mine[e[2]]}
-                blocks = []
-                for a in range(2):
-                    for core in range(2):
-                        blocks.append(r1[r][(a, core) + tuple(all_here[b] for b in left(r, 1))])
-                for a in range(2):
-                    for core in range(2):
-                        blocks.append(r2[r][(a, core) + tuple(all_here[b] for b in left(r, 2))])
-                for b2 in range(2):
-                    for a in range(2):
-                        for core in range(2):
-                            blocks.append(r3[r][(b2, a, core) + tuple(all_here[b] for b in left(r, 3))])
-                x_at = [b[0] for b in e[3:]].index("x")
-                binned = jnp.dot(weights[2 * r + f[x_at]], jnp.concatenate(blocks, axis=0), preferred_element_type=F32)
-                if f[0]:
-                    s4[r][f[1], f[2]] = binned.astype(BF16)
-                else:
-                    k4[r][f[1], f[2]] = binned
-            to = device((e[3],), c)
-            if at == 2:
-                send(s4[r].at[:, v], r4[r].at[:, v], sem4.at[r, v], to)
-            elif at == 1:
-                send(s4[r].at[v], r4[r].at[v], sem4.at[r, v], to)
-            elif v == 1:
-                send(s4[r], r4[r], sem4.at[r, 0], to)
-
-    def step5(r, f5, f6):
+            for u in (1, 0):
+                fix = pick_part(r, v, u)
+                send(
+                    view(r1[r], (every, every), left(r, 1), {e2: mine[e2], e3: other[e3]} | fix),
+                    view(r3[r], (0, every, every), left(r, 3), fix),
+                    sem3.at[r, 2 * v + u],
+                    device((e3,), c),
+                )
+
+    def step3(r, v, u):
+        e1, e2, e3 = bits_of(r)[:3]
+        fix = pick_part(r, v, u)
+        wait(view(r2[r], (every, every), left(r, 2), fix), sem2.at[r, 2 * v + u])
+        send(
+            view(r2[r], (every, every), left(r, 2), {e3: other[e3]} | fix),
+            view(r3[r], (1, every, every), left(r, 3), fix),
+            sem3.at[r, 2 * v + u],
+            device((e3,), c),
+        )
+
+    def step4(r, v, u):
+        e = bits_of(r)
+        first, second = keys(r)
+        wait(view(r3[r], (every,) * 3, left(r, 3), pick_part(r, v, u)), sem3.at[r, 2 * v + u])
+        x_left = [b for b in e[3:] if b[0] == "x"][0]
+        for w in range(2):
+            flip = {b: w for b in e[3:]} | {first: v, second: u}
+            here = {b: (other if flip[b] else mine)[b] for b in e[3:]} | {e[1]: mine[e[1]], e[2]: mine[e[2]]}
+            blocks = []
+            for ref, lead in ((r1[r], 0), (r2[r], 0), (r3[r], 1)):
+                for a in range(4 << lead):
+                    front = ((a >> 2,) if lead else ()) + ((a >> 1) & 1, a & 1)
+                    used = 3 if lead else (1 if ref is r1[r] else 2)
+                    blocks.append(ref[front + tuple(here[b] for b in left(r, used))])
+            table = weights[2 * r + flip[x_left]]
+            binned = jnp.dot(table, jnp.concatenate(blocks, axis=0), preferred_element_type=F32)
+            f4, f5, f6 = (flip[b] for b in e[3:])
+            if f4:
+                s4[r][f5, f6] = binned.astype(BF16)
+            else:
+                k4[r][f5, f6] = binned
+        to = device((e[3],), c)
+        if first == e[3] and v:
+            send(s4[r].at[u], r4[r].at[u], sem4.at[r, u], to)
+        elif first == e[4] and u:
+            send(s4[r].at[v], r4[r].at[v], sem4.at[r, v], to)
+        elif first == e[5] and u:
+            send(s4[r].at[:, v], r4[r].at[:, v], sem4.at[r, v], to)
+
+    def add5(r, f5, f6):
         total = k4[r][f5, f6] + r4[r][f5, f6].astype(F32)
         if f5:
             s5[r][f6] = total.astype(BF16)
         else:
             k5[r][f6] = total
 
-    for v in HALVES:
-        for r in range(6):
-            at = zlast_at(r)
-            to = device((bits_of(r)[4],), c)
-            if at == 2:
-                wait(r4[r].at[:, v], sem4.at[r, v])
-                step5(r, 1, v)
-                send(s5[r].at[v], r5[r].at[v], sem5.at[r, v], to)
-                step5(r, 0, v)
-            elif at == 1:
-                u = 1 - v
-                wait(r4[r].at[u], sem4.at[r, u])
-                step5(r, u, 0)
-                step5(r, u, 1)
-                if u:
-                    send(s5[r], r5[r], sem5.at[r, 0], to)
-            elif v == 1:
-                wait(r4[r], sem4.at[r, 0])
-                step5(r, 1, 0)
-                step5(r, 1, 1)
+    def step5(r, v, u):
+        e, first = bits_of(r), keys(r)[0]
+        to = device((e[4],), c)
+        if first == e[3] and not v:
+            wait(r4[r].at[u], sem4.at[r, u])
+            add5(r, u, 0)
+            add5(r, u, 1)
+            if u:
                 send(s5[r], r5[r], sem5.at[r, 0], to)
-                step5(r, 0, 0)
-                step5(r, 0, 1)
+        elif first == e[4] and not u:
+            wait(r4[r].at[v], sem4.at[r, v])
+            add5(r, v, 0)
+            add5(r, v, 1)
+            if v:
+                send(s5[r], r5[r], sem5.at[r, 0], to)
+        elif first == e[5] and not u:
+            wait(r4[r].at[:, v], sem4.at[r, v])
+            add5(r, 1, v)
+            send(s5[r].at[v], r5[r].at[v], sem5.at[r, v], to)
+            add5(r, 0, v)
+
+    parts = ((1, 1), (1, 0), (0, 1), (0, 0))
+    for n in range(6):
+        for r in range(6):
+            if n < 4:
+                step3(r, *parts[n])
+        for r in range(6):
+            if 1 < n:
+                step4(r, *parts[n - 2])
+        for r in range(6):
+            if 1 < n:
+                step5(r, *parts[n - 2])
 
     for r in range(6):
-        if zlast_at(r) == 2:
+        if keys(r)[0] == bits_of(r)[5]:
             wait(r5[r].at[1], sem5.at[r, 1])
         else:
             wait(r5[r], sem5.at[r, 0])
         s6[r][...] = (k5[r][1] + r5[r][1].astype(F32)).astype(BF16)
         send(s6[r], r6[r], sem6.at[r], device((bits_of(r)[5],), c))
     for r, (h, start, width) in enumerate(STREAMS):
-        if zlast_at(r) == 2:
+        if keys(r)[0] == bits_of(r)[5]:
             wait(r5[r].at[0], sem5.at[r, 0])
         wait(r6[r], sem6.at[r])
         total = k5[r][0] + r5[r][0].astype(F32) + r6[r][...].astype(F32)
@@ -323,7 +332,9 @@
         pltpu.SemaphoreType.DMA((4,)),
         pltpu.SemaphoreType.DMA((4,)),
         pltpu.SemaphoreType.DMA,
-        *[pltpu.SemaphoreType.DMA((6, 2))] * 5,
+        pltpu.SemaphoreType.DMA((6, 2)),
+        *[pltpu.SemaphoreType.DMA((6, 4))] * 2,
+        *[pltpu.SemaphoreType.DMA((6, 2))] * 2,
         pltpu.SemaphoreType.DMA((6,)),
     ]
     smem = pl.BlockSpec(memory_space=pltpu.SMEM)

time: 98.7 us -> 95 us (0.963)
  Pallas kernels: 96.2 us -> 92.4 us
    pallas_call x1, Pallas kernels: 96.2 us -> 92.4 us  [on_device(): pl.pallas_call(kernel, out_shape=jax.ShapeDtypeStruct((rows, 8, width), F...]
where the time goes in v3:
time: 95 us; the launch traced here: 94.8 us
  Pallas kernels  92.4 us (97%)
  local copies, waits for them, and re-layouts  2.31 us (2%)
    pallas_call x1, Pallas kernels, on_device(): pl.pallas_call(kernel, out_shape=jax.ShapeDtypeStruct((rows, 8, width), F...  92.4 us
    unnamed x1, local copies, waits for them, and re-layouts  2.31 us

profile of v3, /device:TPU:1, one launch (start us, length us, event | category | flops | bytes accessed | tf_op | source)
XLA Modules:
  0.0 94.8 jit_solution(16072617871079490399)
XLA Ops:
  0.0 92.4 %shard_map.55 = f32[32,8,1024]{2,1,0:T(8,128)} custom-call(s32[32]{0:T(128)} %owner.1, s32[16,32]{1,0:T(8,128)} %bitcast.6, s32[16,32]{1,0:T(8,128)} %bitcast.7, bf16[1024,1024]{1,0:T(8,128)(2,1)} %bitcast.5, bf16[4,1024,1024]{2,1,0:T(8,128)(2,1)} %bitcast.4), custom_call_target="tpu_custom_call" | custom-call | flops 12999999488 | bytes 12582912 | tf_op jit(solution)/shard_map/pallas_call | solution.py:342
  92.5 2.3 %copy.7 = f32[32,8,1024]{2,1,0:T(8,128)} copy(f32[32,8,1024]{2,1,0:T(8,128)} %shard_map.55) | data formatting | bytes 2097152

commit v4 on v0

v4 whole, which is shorter than its diff:
```python
import jax
import jax.numpy as jnp
from jax import lax
from jax.experimental import pallas as pl
from jax.experimental.pallas import tpu as pltpu
from jax.sharding import PartitionSpec as P

MESH = pl.DeviceIdType.MESH
BF16, F32, I32 = jnp.bfloat16, jnp.float32, jnp.int32
NAT = ("x1", "x0", "z1", "z0", "y1", "y0")
ORDER = ("x0", "y0", "z0", "x1", "y1", "z1")
STREAMS = ((0, 0, 384, 0), (0, 384, 384, 1), (0, 768, 256, 2), (1, 0, 384, 0), (1, 384, 384, 1), (1, 768, 256, 2))
CHUNKS = (1, 2, 3, 0)


def a_bits(q):
    return [axis + str(q) for axis in "xyz"]


def b_bits(r):
    q, first = STREAMS[r][0], STREAMS[r][3]
    return ["xyz"[(first + i) % 3] + str(1 - q) for i in range(3)]


def tables(r):
    ahead = b_bits(r)[0][0] == "x"
    return [(r, a, f) for a in range(2) for f in range(1 if ahead else 2)]


TABLES = [key for r in range(6) for key in tables(r)]


def gray(v):
    return v + v // 2 - 2 * (v // 3)


def view(ref, lead, names, fixed, tail=()):
    return ref.at[tuple(lead) + tuple(fixed[b] if b in fixed else slice(None) for b in names) + tuple(tail)]


def kernel(owner, screen, live, amp_hbm, int_hbm, out, amp, ints, ordered, column, pieces, weights, *rest):
    r1 = rest[:2]
    r3, s4, r4, k4, s5, r5, k5, s6, r6 = (rest[2 + 6 * i : 8 + 6 * i] for i in range(9))
    load_sem, amp_sem, far_sem, send_sem, sem1, sem3, sem4, sem5, sem6 = rest[56:]
    x, t = lax.axis_index("rep"), lax.axis_index("tile")
    z, y, c = t // 8, (t // 2) % 4, t % 2
    g = {"x": gray(x), "y": gray(y), "z": gray(z)}
    mine = {a + "1": g[a] // 2 for a in g} | {a + "0": g[a] % 2 for a in g}
    other = {b: 1 - mine[b] for b in mine}

    def device(flips, core):
        at = {a: gray((other if a + "1" in flips else mine)[a + "1"] * 2 + (other if a + "0" in flips else mine)[a + "0"]) for a in g}
        return (at["z"] * 8 + at["y"] * 2 + core, at["x"])

    sent = []

    def send(src, dst, sem, to):
        copy = pltpu.make_async_remote_copy(src, dst, send_sem, sem, device_id=to, device_id_type=MESH)
        copy.start()
        sent.append(copy)

    def wait(ref, sem):
        pltpu.make_async_copy(ref, ref, sem).wait()

    load_amp = pltpu.make_async_copy(amp_hbm, amp, load_sem.at[0])
    load_amp.start()
    load_ints = [pltpu.make_async_copy(int_hbm.at[j], ints.at[j], load_sem.at[1 + j]) for j in range(4)]

    barrier = pltpu.get_barrier_semaphore()

    @pl.loop(1, 32)
    def _(k):
        to = ((z + k // 8) % 4) * 8 + ((y + (k // 2) % 4) % 4) * 2 + (c + k) % 2
        pl.semaphore_signal(barrier, inc=1, device_id=(to, x), device_id_type=MESH)

    for b in ("x0", "x1"):
        for core in range(2):
            pl.semaphore_signal(barrier, inc=1, device_id=device((b,), core), device_id_type=MESH)
    pl.semaphore_signal(barrier, inc=1, device_id=device(("x0", "x1"), c), device_id_type=MESH)
    for q in range(2):
        pl.semaphore_signal(barrier, inc=1, device_id=device(a_bits(q), c), device_id_type=MESH)

    def far(n):
        return ((2, x // 2), (2, 2 + x // 2), (1, 2 - x // 2), (3, 2 + x // 2))[n] + (x % 2,)

    load_amp.wait()
    for load in load_ints:
        load.start()
    away = lax.broadcasted_iota(I32, (32, 1024), 1) - 32 * lax.broadcasted_iota(I32, (32, 1024), 0)
    own_row = g["y"] * 2 + c
    near = [(dz, dy, dc) for dz, dy in ((1, 0), (1, 3), (3, 0), (3, 1), (0, 1), (0, 3), (0, 0), (0, 2)) for dc in (0, 1)]
    blocks = [far(n) for n in (2, 3, 0, 1)] + near
    for first in (0, 8, 16):
        some = blocks[first : first + 8]
        to = [((z + dz) % 4) * 8 + ((y + dy) % 4) * 2 + (c + dc) % 2 for dz, dy, dc in some]
        pick = [jnp.where(away == owner[p], 1.0, 0.0).astype(BF16) for p in to]
        pick = jnp.concatenate(pick, axis=0)
        for n in range(2):
            got = jnp.dot(pick, amp[:, n * 512 : n * 512 + 512], preferred_element_type=F32)
            ordered[first : first + len(some), :, n * 512 : n * 512 + 512] = got.astype(BF16).reshape(len(some), 32, 512)
        if first == 0:
            pl.semaphore_wait(barrier, 38)
        for i, p in enumerate(to):
            src, dst = ordered.at[first + i], column.at[g["z"], own_row]
            if some[i] == (0, 0, 0):
                pltpu.make_async_copy(src, dst, amp_sem.at[g["z"]]).start()
            elif first == 0 and i < 4:
                send(src, dst, far_sem.at[(2, 3, 0, 1)[i]], (p, x))
            else:
                send(src, dst, amp_sem.at[g["z"]], (p, x))

    lane = lax.broadcasted_iota(I32, (8, 256), 1)
    bin_of_row = lax.broadcasted_iota(I32, (8, 256), 0)
    for n, (r, a, f) in enumerate(TABLES):
        q, b1 = STREAMS[r][0], b_bits(r)[0]
        xa, xb = "x" + str(q), "x" + str(1 - q)
        want = {xa: (other if a else mine)[xa], xb: (other if f else mine)[xb]}
        block = gray(want["x1"] * 2 + want["x0"])
        label = jnp.full((8, 256), -1, I32)
        for s in range(16):
            chip = (s >> 1) & 3
            tile, rep = device(([b1] if s >> 3 else []) + ([a_bits(q)[chip - 1]] if chip else []), s & 1)
            slot = rep * 4 + block
            found = jnp.where(live[slot, tile] != 0, screen[slot, tile] - 8 * block, -1)
            label = jnp.where(lane // 16 == s, found, label)
        hit = label == bin_of_row
        rows = [jnp.where(hit & (lane % 16 == m), 1.0, 0.0).astype(F32) for m in range(16)]
        weights[n] = jnp.concatenate(rows, axis=0).astype(BF16)

    for n in (2, 3, 0, 1):
        dz, dy, dc = far(n)
        gz = gray((z - dz + 4) % 4)
        block = column.at[gz, gray((y - dy + 4) % 4) * 2 + (c + dc) % 2]
        wait(block, far_sem.at[n])
        for dx in (1, 3, 2):
            send(block, block, amp_sem.at[gz], (t, (x + dx) % 4))

    for load in load_ints:
        load.wait()

    for k in CHUNKS:
        zv = {"z1": (other if k >> 1 else mine)["z1"], "z0": (other if k & 1 else mine)["z0"]}
        gz = zv["z1"] * 2 + zv["z0"]
        wait(column.at[gz, pl.ds(0, (8, 7, 7, 6)[k])], amp_sem.at[gz])

        @pl.loop(0, 4)
        def _(j):
            left_side = column[gz].reshape(256, 1024)
            got = jnp.dot(left_side, ints[j], preferred_element_type=F32).astype(BF16)
            gj = gray(j)
            pieces[gj // 2, gj % 2, zv["z1"], zv["z0"]] = got.reshape(2, 2, 2, 2, 16, 1024)

        flip_z = {"z0": k & 1, "z1": k >> 1}
        for q in range(2):
            xa, ya, za = a_bits(q)
            zb = "z" + str(1 - q)
            f = flip_z[za]
            sem = sem1.at[q, flip_z[zb]]

            def part(fx, fy, core):
                at = {xa: (other if fx else mine)[xa], ya: (other if fy else mine)[ya]} | zv
                return view(pieces, (), NAT, at, (core, q))

            def place(chip, a):
                return r1[q].at[chip, c, a, :, zv[zb], :]

            for core in range(2):
                send(part(1 - f, f, core), place(1, f), sem, device((xa,), core))
                send(part(f, 1 - f, core), place(2, f), sem, device((ya,), core))
                send(part(1 - f, 1 - f, core), place(3, 1 - f), sem, device((za,), core))
            send(part(f, f, 1 - c), place(0, f), sem, device((), 1 - c))
            pltpu.make_async_copy(part(f, f, c), place(0, f), sem).start()

    every = slice(None)

    def where(r, f1, f2, f3):
        b1, b2, b3 = b_bits(r)
        return {b: (other if f else mine)[b] for b, f in ((b1, f1), (b2, f2), (b3, f3))}

    def in_r1(r, at):
        q = STREAMS[r][0]
        return tuple(at[axis + str(1 - q)] for axis in "xzy")

    def in_r3(r, at):
        first = b_bits(r)[0]
        return tuple(at[b] for b in (axis + str(1 - STREAMS[r][0]) for axis in "xzy") if b != first)

    def columns(r):
        return pl.ds(STREAMS[r][1], STREAMS[r][2])

    def z_at(r):
        return [b[0] for b in b_bits(r)].index("z")

    halves = ((1, 1), (1, 0), (0, 1), (0, 0))

    def step3(r, a, f2, f3):
        at = where(r, 1, f2, f3)
        src = r1[STREAMS[r][0]].at[(every, every, a) + in_r1(r, at) + (every, columns(r))]
        dst = r3[r].at[(every, every, a) + in_r3(r, at)]
        send(src, dst, sem3.at[r, 4 * a + 2 * f2 + f3], device((b_bits(r)[0],), c))

    for v in (1, 0):
        for q in range(2):
            zb = "z" + str(1 - q)
            wait(r1[q].at[:, :, :, :, (other if v else mine)[zb], :], sem1.at[q, v])
            for a in (1, 0):
                for f2, f3 in halves:
                    for r in range(3 * q, 3 * q + 3):
                        if (1, f2, f3)[z_at(r)] == v:
                            step3(r, a, f2, f3)

    def step4(r, a, f2, f3):
        q = STREAMS[r][0]
        at = where(r, 0, f2, f3)
        wait(r3[r].at[(every, every, a) + in_r3(r, at)], sem3.at[r, 4 * a + 2 * f2 + f3])
        fx = {b_bits(r)[1]: f2, b_bits(r)[2]: f3}.get("x" + str(1 - q), 0)
        blocks = []
        for chip in range(4):
            for core in range(2):
                blocks.append(r1[q][(chip, core, a) + in_r1(r, at) + (every, columns(r))])
        for chip in range(4):
            for core in range(2):
                blocks.append(r3[r][(chip, core, a) + in_r3(r, at)])
        table = weights[TABLES.index((r, a, fx))]
        binned = jnp.dot(table, jnp.concatenate(blocks, axis=0), preferred_element_type=F32)
        if f2:
            s4[r][f3, a] = binned.astype(BF16)
            send(s4[r].at[f3, a], r4[r].at[f3, a], sem4.at[r, 2 * a + f3], device((b_bits(r)[1],), c))
        else:
            k4[r][f3, a] = binned

    def step5(r, a, f3):
        wait(r4[r].at[f3, a], sem4.at[r, 2 * a + f3])
        total = k4[r][f3, a] + r4[r][f3, a].astype(F32)
        if f3:
            s5[r][a] = total.astype(BF16)
            send(s5[r].at[a], r5[r].at[a], sem5.at[r, a], device((b_bits(r)[2],), c))
        else:
            k5[r][a] = total

    def home(r):
        wait(r5[r].at[1], sem5.at[r, 1])
        s6[r][...] = (k5[r][1] + r5[r][1].astype(F32)).astype(BF16)
        send(s6[r], r6[r], sem6.at[r], device(a_bits(STREAMS[r][0]), c))

    for a in (1, 0):
        for n, (f2, f3) in enumerate(halves):
            for r in range(6):
                step4(r, a, f2, f3)
            if f2 == 0:
                for r in range(6):
                    step5(r, a, f3)
            if (a, n) == (0, 1):
                for r in range(6):
                    home(r)
    for r, (q, start, width, _) in enumerate(STREAMS):
        wait(r5[r].at[0], sem5.at[r, 0])
        wait(r6[r], sem6.at[r])
        total = k5[r][0] + r5[r][0].astype(F32) + r6[r][...].astype(F32)
        out[16 * q : 16 * q + 16, :, start : start + width] = total.reshape(16, 8, width)

    for copy in sent:
        copy.wait_send()


def on_device(amplitudes, integrals, owner_order, screen_list, live_mask):
    rows, tiles, width = amplitudes.shape
    widths = [w for _, _, w, _ in STREAMS]

    def group(lead, tail, dtype):
        return [pltpu.VMEM(lead + tail(w), dtype) for w in widths]

    two = (2,)
    raw = lambda w: (16, w)
    dense = lambda w: (128, w)
    scratch = [
        pltpu.VMEM((rows * tiles, width), BF16),
        pltpu.VMEM((4, width, width), BF16),
        pltpu.VMEM((20, rows, width), BF16),
        pltpu.VMEM((4, 8, rows, width), BF16),
        pltpu.VMEM(two * 8 + (16, width), BF16),
        pltpu.VMEM((len(TABLES), 128, 256), BF16),
        *[pltpu.VMEM((4, 2, 2, 2, 2, 2, 16, width), BF16)] * 2,
        *group((4, 2, 2, 2, 2), raw, BF16),
        *group(two * 2, dense, BF16),
        *group(two * 2, dense, BF16),
        *group(two * 2, dense, F32),
        *group(two, dense, BF16),
        *group(two, dense, BF16),
        *group(two, dense, F32),
        *group((), dense, BF16),
        *group((), dense, BF16),
        pltpu.SemaphoreType.DMA((5,)),
        pltpu.SemaphoreType.DMA((4,)),
        pltpu.SemaphoreType.DMA((4,)),
        pltpu.SemaphoreType.DMA,
        pltpu.SemaphoreType.DMA((2, 2)),
        pltpu.SemaphoreType.DMA((6, 8)),
        pltpu.SemaphoreType.DMA((6, 4)),
        pltpu.SemaphoreType.DMA((6, 2)),
        pltpu.SemaphoreType.DMA((6,)),
    ]
    smem = pl.BlockSpec(memory_space=pltpu.SMEM)
    hbm = pl.BlockSpec(memory_space=pl.ANY)
    return pl.pallas_call(
        kernel,
        out_shape=jax.ShapeDtypeStruct((rows, 8, width), F32),
        in_specs=[smem, smem, smem, hbm, hbm],
        out_specs=pl.BlockSpec(memory_space=pltpu.VMEM),
        scratch_shapes=scratch,
        cost_estimate=pl.CostEstimate(flops=13_000_000_000, bytes_accessed=12 << 20, transcendentals=0),
        compiler_params=pltpu.CompilerParams(
            collective_id=0, has_side_effects=True, vmem_limit_bytes=60 << 20
        ),
    )(owner_order, screen_list.T, live_mask.T, amplitudes.reshape(rows * tiles, width), integrals[0])


def solution(mesh):
    in_specs = (P("tile", None, None), P("tile", "rep", None, None), P(), P(), P())
    out_specs = P("tile", "rep", None)
    return jax.shard_map(
        on_device, mesh=mesh, in_specs=in_specs, out_specs=out_specs, check_vma=False
    )
```

time: 252 us -> 90.6 us (0.36)
  waiting for transfers between devices: 175 us -> 0 us
  Pallas kernels: 0 us -> 87.6 us
  matrix products: 23.2 us -> 0 us
  starting transfers between devices: 16.7 us -> 0 us
  local copies, waits for them, and re-layouts: 18.8 us -> 2.31 us
  between operations: 13.4 us -> 0.01 us
  other arithmetic: 4.21 us -> 0 us
    all_to_all x2 -> x0, waiting for transfers between devices: 126 us -> none  [the longest x1 99 us: on_device(): lax.all_to_all(grouped, 'tile', split_axis=0, concat_axis=0, tiled=True)]
    pallas_call x0 -> x1, Pallas kernels: none -> 87.6 us  [on_device(): pl.pallas_call(kernel, out_shape=jax.ShapeDtypeStruct((rows, 8, width), F...]
    reduce_scatter x1 -> x0, waiting for transfers between devices: 49.5 us -> none  [on_device(): return lax.psum_scatter(dense_sum, 'rep', scatter_dimension=1, tiled=True)]
    dot_general x2 -> x0, matrix products: 23.2 us -> none  [the longest x1 12.8 us: on_device(): jnp.einsum('mc,scd->msd', column, integrals[0], preferred_element_type=jn...]
    all_to_all x2 -> x0, starting transfers between devices: 16.7 us -> none  [the longest x1 9.67 us: on_device(): lax.all_to_all(ordered, 'tile', split_axis=1, concat_axis=0, tiled=True)]
    gather x1 -> x0, local copies, waits for them, and re-layouts: 7.88 us -> none  [on_device(): ordered = jnp.take(amplitudes, owner_order, axis=1)]
    reshape x1 -> x0, local copies, waits for them, and re-layouts: 7.65 us -> none  [on_device(): pieces.astype(jnp.bfloat16)]
    select_n x2 -> x0, other arithmetic: 2.66 us -> none  [on_device(): ordered = jnp.take(amplitudes, owner_order, axis=1)]
  transfers between devices with their start and end apart: 3 -> 0, of which waited for: 3 -> 0; matrix products, arithmetic and copies ran while one was open for 1% -> 0% of each run, Pallas kernels for 0% -> 0%
where the time goes in v4:
time: 90.6 us; the launch traced here: 89.9 us
  Pallas kernels  87.6 us (97%)
  local copies, waits for them, and re-layouts  2.31 us (3%)
    pallas_call x1, Pallas kernels, on_device(): pl.pallas_call(kernel, out_shape=jax.ShapeDtypeStruct((rows, 8, width), F...  87.6 us
    unnamed x1, local copies, waits for them, and re-layouts  2.31 us

profile of v4, /device:TPU:1, one launch (start us, length us, event | category | flops | bytes accessed | tf_op | source)
XLA Modules:
  0.0 89.9 jit_solution(9336436479669977170)
XLA Ops:
  0.0 87.6 %shard_map.55 = f32[32,8,1024]{2,1,0:T(8,128)} custom-call(s32[32]{0:T(128)} %owner.1, s32[16,32]{1,0:T(8,128)} %bitcast.6, s32[16,32]{1,0:T(8,128)} %bitcast.7, bf16[1024,1024]{1,0:T(8,128)(2,1)} %bitcast.5, bf16[4,1024,1024]{2,1,0:T(8,128)(2,1)} %bitcast.4), custom_call_target="tpu_custom_call" | custom-call | flops 12999999488 | bytes 12582912 | tf_op jit(solution)/shard_map/pallas_call | solution.py:305
  87.6 2.3 %copy.7 = f32[32,8,1024]{2,1,0:T(8,128)} copy(f32[32,8,1024]{2,1,0:T(8,128)} %shard_map.55) | data formatting | bytes 2097152

commit v5 on v4

--- a/solution.py
+++ b/solution.py
@@ -203,11 +203,10 @@
         for q in range(2):
             zb = "z" + str(1 - q)
             wait(r1[q].at[:, :, :, :, (other if v else mine)[zb], :], sem1.at[q, v])
-            for a in (1, 0):
-                for f2, f3 in halves:
-                    for r in range(3 * q, 3 * q + 3):
-                        if (1, f2, f3)[z_at(r)] == v:
-                            step3(r, a, f2, f3)
+            for f2, f3 in halves:
+                for r in range(3 * q, 3 * q + 3):
+                    if (1, f2, f3)[z_at(r)] == v:
+                        step3(r, 1, f2, f3)
 
     def step4(r, a, f2, f3):
         q = STREAMS[r][0]
@@ -243,6 +242,9 @@
         s6[r][...] = (k5[r][1] + r5[r][1].astype(F32)).astype(BF16)
         send(s6[r], r6[r], sem6.at[r], device(a_bits(STREAMS[r][0]), c))
 
+    for n in range(1):
+        for r in range(6):
+            step3(r, 0, *halves[n])
     for a in (1, 0):
         for n, (f2, f3) in enumerate(halves):
             for r in range(6):
@@ -250,6 +252,9 @@
             if f2 == 0:
                 for r in range(6):
                     step5(r, a, f3)
+            if a and n + 1 < 4:
+                for r in range(6):
+                    step3(r, 0, *halves[n + 1])
             if (a, n) == (0, 1):
                 for r in range(6):
                     home(r)

time: 90.6 us -> 89.1 us (0.983)
  Pallas kernels: 87.6 us -> 85.7 us
    pallas_call x1, Pallas kernels: 87.6 us -> 85.7 us  [on_device(): pl.pallas_call(kernel, out_shape=jax.ShapeDtypeStruct((rows, 8, width), F...]
where the time goes in v5:
time: 89.1 us; the launch traced here: 88 us
  Pallas kernels  85.7 us (96%)
  local copies, waits for them, and re-layouts  2.31 us (3%)
    pallas_call x1, Pallas kernels, on_device(): pl.pallas_call(kernel, out_shape=jax.ShapeDtypeStruct((rows, 8, width), F...  85.7 us
    unnamed x1, local copies, waits for them, and re-layouts  2.31 us

profile of v5, /device:TPU:1, one launch (start us, length us, event | category | flops | bytes accessed | tf_op | source)
XLA Modules:
  0.0 88.0 jit_solution(8539335884244628451)
XLA Ops:
  0.0 85.7 %shard_map.55 = f32[32,8,1024]{2,1,0:T(8,128)} custom-call(s32[32]{0:T(128)} %owner.1, s32[16,32]{1,0:T(8,128)} %bitcast.6, s32[16,32]{1,0:T(8,128)} %bitcast.7, bf16[1024,1024]{1,0:T(8,128)(2,1)} %bitcast.5, bf16[4,1024,1024]{2,1,0:T(8,128)(2,1)} %bitcast.4), custom_call_target="tpu_custom_call" | custom-call | flops 12999999488 | bytes 12582912 | tf_op jit(solution)/shard_map/pallas_call | solution.py:310
  85.7 2.3 %copy.7 = f32[32,8,1024]{2,1,0:T(8,128)} copy(f32[32,8,1024]{2,1,0:T(8,128)} %shard_map.55) | data formatting | bytes 2097152

commit v6 on v5

--- a/solution.py
+++ b/solution.py
@@ -109,6 +109,78 @@
             else:
                 send(src, dst, amp_sem.at[g["z"]], (p, x))
 
+    for n in (2, 3, 0, 1):
+        dz, dy, dc = far(n)
+        gz = gray((z - dz + 4) % 4)
+        block = column.at[gz, gray((y - dy + 4) % 4) * 2 + (c + dc) % 2]
+        wait(block, far_sem.at[n])
+        for dx in (1, 3, 2):
+            send(block, block, amp_sem.at[gz], (t, (x + dx) % 4))
+
+    for load in load_ints:
+        load.wait()
+
+    for k in CHUNKS:
+        zv = {"z1": (other if k >> 1 else mine)["z1"], "z0": (other if k & 1 else mine)["z0"]}
+        gz = zv["z1"] * 2 + zv["z0"]
+        wait(column.at[gz, pl.ds(0, (8, 7, 7, 6)[k])], amp_sem.at[gz])
+
+        @pl.loop(0, 4)
+        def _(j):
+            left_side = column[gz].reshape(256, 1024)
+            got = jnp.dot(left_side, ints[j], preferred_element_type=F32).astype(BF16)
+            gj = gray(j)
+            pieces[gj // 2, gj % 2, zv["z1"], zv["z0"]] = got.reshape(2, 2, 2, 2, 16, 1024)
+
+        flip_z = {"z0": k & 1, "z1": k >> 1}
+        for q in range(2):
+            xa, ya, za = a_bits(q)
+            zb = "z" + str(1 - q)
+            f = flip_z[za]
+            sem = sem1.at[q, flip_z[zb]]
+
+            def part(fx, fy, core):
+                at = {xa: (other if fx else mine)[xa], ya: (other if fy else mine)[ya]} | zv
+                return view(pieces, (), NAT, at, (core, q))
+
+            def place(chip, a):
+                return r1[q].at[chip, c, a, :, zv[zb], :]
+
+            for core in range(2):
+                send(part(1 - f, f, core), place(1, f), sem, device((xa,), core))
+                send(part(f, 1 - f, core), place(2, f), sem, device((ya,), core))
+                send(part(1 - f, 1 - f, core), place(3, 1 - f), sem, device((za,), core))
+            send(part(f, f, 1 - c), place(0, f), sem, device((), 1 - c))
+            pltpu.make_async_copy(part(f, f, c), place(0, f), sem).start()
+
+    every = slice(None)
+
+    def where(r, f1, f2, f3):
+        b1, b2, b3 = b_bits(r)
+        return {b: (other if f else mine)[b] for b, f in ((b1, f1), (b2, f2), (b3, f3))}
+
+    def in_r1(r, at):
+        q = STREAMS[r][0]
+        return tuple(at[axis + str(1 - q)] for axis in "xzy")
+
+    def in_r3(r, at):
+        first = b_bits(r)[0]
+        return tuple(at[b] for b in (axis + str(1 - STREAMS[r][0]) for axis in "xzy") if b != first)
+
+    def columns(r):
+        return pl.ds(STREAMS[r][1], STREAMS[r][2])
+
+    def z_at(r):
+        return [b[0] for b in b_bits(r)].index("z")
+
+    halves = ((1, 1), (1, 0), (0, 1), (0, 0))
+
+    def step3(r, a, f2, f3):
+        at = where(r, 1, f2, f3)
+        src = r1[STREAMS[r][0]].at[(every, every, a) + in_r1(r, at) + (every, columns(r))]
+        dst = r3[r].at[(every, every, a) + in_r3(r, at)]
+        send(src, dst, sem3.at[r, 4 * a + 2 * f2 + f3], device((b_bits(r)[0],), c))
+
     lane = lax.broadcasted_iota(I32, (8, 256), 1)
     bin_of_row = lax.broadcasted_iota(I32, (8, 256), 0)
     for n, (r, a, f) in enumerate(TABLES):
@@ -126,78 +198,6 @@
         hit = label == bin_of_row
         rows = [jnp.where(hit & (lane % 16 == m), 1.0, 0.0).astype(F32) for m in range(16)]
         weights[n] = jnp.concatenate(rows, axis=0).astype(BF16)
-
-    for n in (2, 3, 0, 1):
-        dz, dy, dc = far(n)
-        gz = gray((z - dz + 4) % 4)
-        block = column.at[gz, gray((y - dy + 4) % 4) * 2 + (c + dc) % 2]
-        wait(block, far_sem.at[n])
-        for dx in (1, 3, 2):
-            send(block, block, amp_sem.at[gz], (t, (x + dx) % 4))
-
-    for load in load_ints:
-        load.wait()
-
-    for k in CHUNKS:
-        zv = {"z1": (other if k >> 1 else mine)["z1"], "z0": (other if k & 1 else mine)["z0"]}
-        gz = zv["z1"] * 2 + zv["z0"]
-        wait(column.at[gz, pl.ds(0, (8, 7, 7, 6)[k])], amp_sem.at[gz])
-
-        @pl.loop(0, 4)
-        def _(j):
-            left_side = column[gz].reshape(256, 1024)
-            got = jnp.dot(left_side, ints[j], preferred_element_type=F32).astype(BF16)
-            gj = gray(j)
-            pieces[gj // 2, gj % 2, zv["z1"], zv["z0"]] = got.reshape(2, 2, 2, 2, 16, 1024)
-
-        flip_z = {"z0": k & 1, "z1": k >> 1}
-        for q in range(2):
-            xa, ya, za = a_bits(q)
-            zb = "z" + str(1 - q)
-            f = flip_z[za]
-            sem = sem1.at[q, flip_z[zb]]
-
-            def part(fx, fy, core):
-                at = {xa: (other if fx else mine)[xa], ya: (other if fy else mine)[ya]} | zv
-                return view(pieces, (), NAT, at, (core, q))
-
-            def place(chip, a):
-                return r1[q].at[chip, c, a, :, zv[zb], :]
-
-            for core in range(2):
-                send(part(1 - f, f, core), place(1, f), sem, device((xa,), core))
-                send(part(f, 1 - f, core), place(2, f), sem, device((ya,), core))
-                send(part(1 - f, 1 - f, core), place(3, 1 - f), sem, device((za,), core))
-            send(part(f, f, 1 - c), place(0, f), sem, device((), 1 - c))
-            pltpu.make_async_copy(part(f, f, c), place(0, f), sem).start()
-
-    every = slice(None)
-
-    def where(r, f1, f2, f3):
-        b1, b2, b3 = b_bits(r)
-        return {b: (other if f else mine)[b] for b, f in ((b1, f1), (b2, f2), (b3, f3))}
-
-    def in_r1(r, at):
-        q = STREAMS[r][0]
-        return tuple(at[axis + str(1 - q)] for axis in "xzy")
-
-    def in_r3(r, at):
-        first = b_bits(r)[0]
-        return tuple(at[b] for b in (axis + str(1 - STREAMS[r][0]) for axis in "xzy") if b != first)
-
-    def columns(r):
-        return pl.ds(STREAMS[r][1], STREAMS[r][2])
-
-    def z_at(r):
-        return [b[0] for b in b_bits(r)].index("z")
-
-    halves = ((1, 1), (1, 0), (0, 1), (0, 0))
-
-    def step3(r, a, f2, f3):
-        at = where(r, 1, f2, f3)
-        src = r1[STREAMS[r][0]].at[(every, every, a) + in_r1(r, at) + (every, columns(r))]
-        dst = r3[r].at[(every, every, a) + in_r3(r, at)]
-        send(src, dst, sem3.at[r, 4 * a + 2 * f2 + f3], device((b_bits(r)[0],), c))
 
     for v in (1, 0):
         for q in range(2):
@@ -249,12 +249,11 @@
         for n, (f2, f3) in enumerate(halves):
             for r in range(6):
                 step4(r, a, f2, f3)
+                if a and n + 1 < 4:
+                    step3(r, 0, *halves[n + 1])
             if f2 == 0:
                 for r in range(6):
                     step5(r, a, f3)
-            if a and n + 1 < 4:
-                for r in range(6):
-                    step3(r, 0, *halves[n + 1])
             if (a, n) == (0, 1):
                 for r in range(6):
                     home(r)

time: 89.1 us -> 89 us (level)
  no operation moved by 1% of the time
where the time goes in v6:
time: 89 us; the launch traced here: 88.8 us
  Pallas kernels  86.4 us (97%)
  local copies, waits for them, and re-layouts  2.31 us (3%)
    pallas_call x1, Pallas kernels, on_device(): pl.pallas_call(kernel, out_shape=jax.ShapeDtypeStruct((rows, 8, width), F...  86.4 us
    unnamed x1, local copies, waits for them, and re-layouts  2.31 us

profile of v6, /device:TPU:1, one launch (start us, length us, event | category | flops | bytes accessed | tf_op | source)
XLA Modules:
  0.0 88.8 jit_solution(7474288642221630563)
XLA Ops:
  0.0 86.4 %shard_map.55 = f32[32,8,1024]{2,1,0:T(8,128)} custom-call(s32[32]{0:T(128)} %owner.1, s32[16,32]{1,0:T(8,128)} %bitcast.6, s32[16,32]{1,0:T(8,128)} %bitcast.7, bf16[1024,1024]{1,0:T(8,128)(2,1)} %bitcast.5, bf16[4,1024,1024]{2,1,0:T(8,128)(2,1)} %bitcast.4), custom_call_target="tpu_custom_call" | custom-call | flops 12999999488 | bytes 12582912 | tf_op jit(solution)/shard_map/pallas_call | solution.py:309
  86.5 2.3 %copy.7 = f32[32,8,1024]{2,1,0:T(8,128)} copy(f32[32,8,1024]{2,1,0:T(8,128)} %shard_map.55) | data formatting | bytes 2097152

commit v7 on v5

--- a/solution.py
+++ b/solution.py
@@ -242,7 +242,7 @@
         s6[r][...] = (k5[r][1] + r5[r][1].astype(F32)).astype(BF16)
         send(s6[r], r6[r], sem6.at[r], device(a_bits(STREAMS[r][0]), c))
 
-    for n in range(1):
+    for n in range(0):
         for r in range(6):
             step3(r, 0, *halves[n])
     for a in (1, 0):
@@ -252,9 +252,9 @@
             if f2 == 0:
                 for r in range(6):
                     step5(r, a, f3)
-            if a and n + 1 < 4:
+            if a and n + 0 < 4:
                 for r in range(6):
-                    step3(r, 0, *halves[n + 1])
+                    step3(r, 0, *halves[n + 0])
             if (a, n) == (0, 1):
                 for r in range(6):
                     home(r)

time: 89.1 us -> 89.1 us (level)
  no operation moved by 1% of the time
where the time goes in v7:
time: 89.1 us; the launch traced here: 88 us
  Pallas kernels  85.7 us (96%)
  local copies, waits for them, and re-layouts  2.31 us (3%)
    pallas_call x1, Pallas kernels, on_device(): pl.pallas_call(kernel, out_shape=jax.ShapeDtypeStruct((rows, 8, width), F...  85.7 us
    unnamed x1, local copies, waits for them, and re-layouts  2.31 us

profile of v7, /device:TPU:1, one launch (start us, length us, event | category | flops | bytes accessed | tf_op | source)
XLA Modules:
  0.0 88.0 jit_solution(133422735009248860)
XLA Ops:
  0.0 85.7 %shard_map.55 = f32[32,8,1024]{2,1,0:T(8,128)} custom-call(s32[32]{0:T(128)} %owner.1, s32[16,32]{1,0:T(8,128)} %bitcast.6, s32[16,32]{1,0:T(8,128)} %bitcast.7, bf16[1024,1024]{1,0:T(8,128)(2,1)} %bitcast.5, bf16[4,1024,1024]{2,1,0:T(8,128)(2,1)} %bitcast.4), custom_call_target="tpu_custom_call" | custom-call | flops 12999999488 | bytes 12582912 | tf_op jit(solution)/shard_map/pallas_call | solution.py:310
  85.7 2.3 %copy.7 = f32[32,8,1024]{2,1,0:T(8,128)} copy(f32[32,8,1024]{2,1,0:T(8,128)} %shard_map.55) | data formatting | bytes 2097152
